TPU v7x, 32 devices: a whole 2x2x4 slice. The times are simulated.
32 devices in a mesh: expert: 16 (over z, x, core), dp: 2 (over y).
Axes of the slice: x: 2, y: 2, z: 4, core: 2. Of those that a mesh axis runs over, the one named last changes fastest.
Arguments:
- tokens: bfloat16 [4096, 6144], P('expert', 'dp'), may hold values from -6 to 6
- grad_out: bfloat16 [4096, 6144], P('expert', 'dp'), may hold values from -0.625 to 0.625
- combine: bfloat16 [4096, 2], P('expert'), may hold values from 0.049804688 to 1
- routes: int32 [4096, 2], P('expert'), may hold values from 0 to 15, all different within a row; in each aligned block of 256 rows (0 to 255, 256 to 511, ...) at most 36 rows name the same one
- w_gate: bfloat16 [16, 256, 6144], P('expert', None, 'dp'), may hold values from -0.078125 to 0.078125
- w_up: bfloat16 [16, 256, 6144], P('expert', None, 'dp'), may hold values from -0.078125 to 0.078125
- w_down: bfloat16 [16, 256, 6144], P('expert', None, 'dp'), may hold values from -0.375 to 0.375
Outputs:
- grad_gate: bfloat16 [16, 256, 6144], P('expert', None, 'dp')
- grad_up: bfloat16 [16, 256, 6144], P('expert', None, 'dp')
- grad_down: bfloat16 [16, 256, 6144], P('expert', None, 'dp')
- grad_combine: float32 [4096, 2], P('expert')
Inputs may be any that keep to these rules, and one draw needn't show every extreme that they name: `routes`: each token names 2 different experts. Among the tokens of one index of the expert axis no expert is named by more than 36 tokens, and on some index one expert is named by exactly 36 tokens.
All inputs are finite; a program needn't handle non-finite values.
Results may differ from a plain program's by a relative error of at most 0.0049.
Values may be sent and summed in bfloat16 or wider, within the bound.
A program may use at most 64 MiB of HBM per device.

v0:
```python
import jax
import jax.numpy as jnp
from jax import lax
from jax.sharding import PartitionSpec as P

inner_dims = (((1,), (1,)), ((), ()))
outer_dims = (((0,), (0,)), ((), ()))


def silu_parts(gate_pre):
    sig_val = jax.nn.sigmoid(gate_pre)
    return (gate_pre * sig_val, sig_val * (1.0 + gate_pre * (1.0 - sig_val)))


def row_terms(gate_pre, up_pre, grad_hid, rows_p):
    silu_out, silu_slope = silu_parts(gate_pre)
    hidden = silu_out * up_pre
    weight = rows_p.astype(jnp.float32)[:, None]
    weighted = (weight * hidden).astype(jnp.bfloat16)
    scaled = weight * grad_hid
    up_rows = (scaled * silu_out).astype(jnp.bfloat16)
    gate_rows = (scaled * up_pre * silu_slope).astype(jnp.bfloat16)
    scores = jnp.sum(hidden * grad_hid, axis=1)
    return (gate_rows, up_rows, weighted, scores)


def local(tokens, grad_out, combine, routes, w_gate, w_up, w_down):
    tok_count, col_width = tokens.shape
    top_count = routes.shape[1]
    expert_count = lax.axis_size("expert")
    capacity = max(2, (9 * tok_count * top_count + 8 * expert_count - 1) // (8 * expert_count))
    assigned = tok_count * top_count
    slot_rows = expert_count * capacity
    flat_expert = routes.reshape(-1)
    onehot = (flat_expert[:, None] == jnp.arange(expert_count, dtype=jnp.int32)[None, :]).astype(
        jnp.int32
    )
    before = jnp.cumsum(onehot, axis=0) - onehot
    ranking = jnp.sum(before * onehot, axis=1)
    slot_of = flat_expert * capacity + ranking
    matches = slot_of[None, :] == jnp.arange(slot_rows, dtype=jnp.int32)[:, None]
    filled = jnp.any(matches, axis=1)
    source = jnp.sum(jnp.where(matches, jnp.arange(assigned, dtype=jnp.int32)[None, :], 0), axis=1)
    token_of = source // top_count
    zero_value = jnp.zeros((), jnp.bfloat16)
    tok_slots = jnp.where(filled[:, None], tokens[token_of], zero_value).reshape(
        expert_count, capacity, col_width
    )
    grad_slots = jnp.where(filled[:, None], grad_out[token_of], zero_value).reshape(
        expert_count, capacity, col_width
    )
    prob_slots = jnp.where(filled, combine.reshape(-1)[source], zero_value).reshape(
        expert_count, capacity
    )
    recv_x, recv_dy, recv_p = (
        lax.all_to_all(tok_slots, "expert", split_axis=0, concat_axis=0, tiled=True),
        lax.all_to_all(grad_slots, "expert", split_axis=0, concat_axis=0, tiled=True),
        lax.all_to_all(prob_slots, "expert", split_axis=0, concat_axis=0, tiled=True),
    )
    rows_x = recv_x.reshape(slot_rows, col_width)
    rows_dy = recv_dy.reshape(slot_rows, col_width)
    rows_p = recv_p.reshape(slot_rows)
    gate_w, up_w, down_w = (w_gate[0], w_up[0], w_down[0])
    gate_pre = lax.dot_general(rows_x, gate_w, inner_dims, preferred_element_type=jnp.float32)
    up_pre = lax.dot_general(rows_x, up_w, inner_dims, preferred_element_type=jnp.float32)
    grad_hid = lax.dot_general(rows_dy, down_w, inner_dims, preferred_element_type=jnp.float32)
    gate_sum, up_sum, grad_sum = lax.psum((gate_pre, up_pre, grad_hid), "dp")
    gate_rows, up_rows, weighted, scores = row_terms(gate_sum, up_sum, grad_sum, rows_p)
    outputs = (
        lax.dot_general(gate_rows, rows_x, outer_dims, preferred_element_type=jnp.float32),
        lax.dot_general(up_rows, rows_x, outer_dims, preferred_element_type=jnp.float32),
        lax.dot_general(weighted, rows_dy, outer_dims, preferred_element_type=jnp.float32),
    )
    returned = lax.all_to_all(
        scores.reshape(expert_count, capacity), "expert", split_axis=0, concat_axis=0, tiled=True
    )
    grad_combine = returned.reshape(-1)[slot_of].reshape(tok_count, top_count)
    return tuple((matrix.astype(jnp.bfloat16)[None] for matrix in outputs)) + (grad_combine,)


def solution(mesh):
    placed = (
        P("expert", "dp"),
        P("expert", "dp"),
        P("expert", None),
        P("expert", None),
        P("expert", None, "dp"),
        P("expert", None, "dp"),
        P("expert", None, "dp"),
    )
    return jax.shard_map(
        local,
        mesh=mesh,
        in_specs=placed,
        out_specs=(
            P("expert", None, "dp"),
            P("expert", None, "dp"),
            P("expert", None, "dp"),
            P("expert", None),
        ),
        check_vma=False,
    )
```

profile of v0, /device:TPU:19, one launch (start us, length us, event | category | flops | bytes accessed | tf_op | source)
XLA Modules:
  0.0 315.1 jit_solution(15449175880517538980)
XLA Ops:
  7.2 0.9 copy.24
  8.4 1.2 reduce-window.6
  10.5 4.6 %gather_fusion.2 = bf16[576,3072]{1,0:T(8,128)(2,1)} fusion(bf16[256,3072]{1,0:T(8,128)(2,1)S(1)} %copy-done, s32[1024]{0:T(1024)S(1)} %get-tuple-element.23), kind=kCustom, calls=%fused_computation.2 | custom fusion | bytes 7080192 | tf_op jit(solution)/shard_map/gather | solution.py:46
  15.1 4.8 %gather.20 = bf16[16,36,3072]{2,1,0:T(8,128)(2,1)} reshape(bf16[576,3072]{1,0:T(8,128)(2,1)} %gather_fusion.2) | data formatting | bytes 7077888 | tf_op jit(solution)/shard_map/gather | solution.py:46
  19.9 4.6 %gather_fusion.1 = bf16[576,3072]{1,0:T(8,128)(2,1)} fusion(bf16[256,3072]{1,0:T(8,128)(2,1)S(1)} %copy-done.1, s32[1024]{0:T(1024)S(1)} %get-tuple-element.23), kind=kCustom, calls=%fused_computation.1 | custom fusion | bytes 7080192 | tf_op jit(solution)/shard_map/gather | solution.py:49
  24.5 4.8 %gather.18 = bf16[16,36,3072]{2,1,0:T(8,128)(2,1)} reshape(bf16[576,3072]{1,0:T(8,128)(2,1)} %gather_fusion.1) | data formatting | bytes 7077888 | tf_op jit(solution)/shard_map/gather | solution.py:49
  29.2 4.9 %broadcast_select_fusion.1 = (bf16[16,36,3072]{2,1,0:T(8,128)(2,1)}, bf16[16,36,3072]{2,1,0:T(8,128)(2,1)S(1)}) fusion(bf16[16,36,3072]{2,1,0:T(8,128)(2,1)} %gather.18, pred[16,36]{1,0:T(8,128)(4,1)S(1)} %broadcast_in_dim.57, bf16[16,36,3072]{2,1,0:T(8,128)(2,1)} %gather.20), kind=kLoop, calls=%fused_computation.5 | loop fusion | flops 3538944 | bytes 14156352 | tf_op jit(solution)/shard_map/jit(_where)/select_n | solution.py:49
  34.2 92.0 %all_to_all.25 = bf16[16,36,3072]{2,1,0:T(8,128)(2,1)} all-to-all(bf16[16,36,3072]{2,1,0:T(8,128)(2,1)S(1)} %get-tuple-element.22), channel_id=1, replica_groups=mesh['expert'=16,'dp'=2] {'expert'}, dimensions={0} | all-to-all | bytes 7077888 | tf_op jit(solution)/shard_map/all_to_all | solution.py:56
  126.2 6.4 %all-to-all-start.1 = ((bf16[16,36,3072]{2,1,0:T(8,128)(2,1)}), bf16[16,36,3072]{2,1,0:T(8,128)(2,1)}, u32[]{:S(2)}, u32[]{:S(2)}) async-start(bf16[16,36,3072]{2,1,0:T(8,128)(2,1)} %get-tuple-element.21), calls=%async_computation.1 | async-start | bytes 7864320 | tf_op jit(solution)/shard_map/all_to_all | solution.py:57
  132.6 4.8 %reshape.203 = bf16[576,3072]{1,0:T(8,128)(2,1)} reshape(bf16[16,36,3072]{2,1,0:T(8,128)(2,1)} %all_to_all.25) | data formatting | bytes 7077888 | tf_op jit(solution)/shard_map/reshape | solution.py:60
  137.4 4.1 %fusion.3 = f32[576,256]{1,0:T(8,128)} fusion(bf16[576,3072]{1,0:T(8,128)(2,1)} %reshape.203, bf16[1,256,3072]{2,1,0:T(8,128)(2,1)S(1)} %copy-done.9), kind=kOutput, calls=%fused_computation.12 | convolution fusion | flops 905969664 | bytes 5701632 | tf_op jit(solution)/shard_map/dot_general | solution.py:64
  141.5 1.9 fusion.5
  143.5 73.8 %all-to-all-done.1 = bf16[16,36,3072]{2,1,0:T(8,128)(2,1)} async-done(((bf16[16,36,3072]{2,1,0:T(8,128)(2,1)}), bf16[16,36,3072]{2,1,0:T(8,128)(2,1)}, u32[]{:S(2)}, u32[]{:S(2)}) %all-to-all-start.1) | async-done | bytes 3538976 | tf_op jit(solution)/shard_map/all_to_all | solution.py:57
  217.3 4.7 %reshape.202 = bf16[576,3072]{1,0:T(8,128)(2,1)} reshape(bf16[16,36,3072]{2,1,0:T(8,128)(2,1)} %all-to-all-done.1) | data formatting | bytes 7077888 | tf_op jit(solution)/shard_map/reshape | solution.py:61
  222.0 4.0 %fusion.7 = f32[576,256]{1,0:T(8,128)} fusion(bf16[576,3072]{1,0:T(8,128)(2,1)} %reshape.202, bf16[1,256,3072]{2,1,0:T(8,128)(2,1)S(1)} %copy-done.11), kind=kOutput, calls=%fused_computation.16 | convolution fusion | flops 905969664 | bytes 5701632 | tf_op jit(solution)/shard_map/dot_general | solution.py:66
  226.3 3.9 %gather_fusion = bf16[576]{0:T(1024)(128)(2,1)S(1)} fusion(bf16[512]{0:T(512)(128)(2,1)S(1)} %reshape.201, s32[1024]{0:T(1024)S(1)} %get-tuple-element.24), kind=kCustom, calls=%fused_computation | custom fusion | bytes 4608 | tf_op jit(solution)/shard_map/gather | solution.py:52
  231.0 7.0 %all-to-all-start = ((bf16[16,1,36]{2,1,0:T(2,128)(2,1)}), bf16[16,1,36]{2,1,0:T(2,128)(2,1)S(1)}, u32[]{:S(2)}, u32[]{:S(2)}) async-start(bf16[16,1,36]{2,1,0:T(2,128)(2,1)} %select_n.80), calls=%async_computation | async-start | bytes 16384 | tf_op jit(solution)/shard_map/all_to_all | solution.py:58
  238.3 3.0 all-to-all-done
  241.4 42.5 %all-reduce.3.cloned.1.call-done = (f32[576,256]{1,0:T(8,128)}, f32[576,256]{1,0:T(8,128)}, f32[576,256]{1,0:T(8,128)}) async-done(((f32[576,256]{1,0:T(8,128)}, f32[576,256]{1,0:T(8,128)}, f32[576,256]{1,0:T(8,128)}), (f32[576,256]{1,0:T(8,128)}, f32[576,256]{1,0:T(8,128)}, f32[576,256]{1,0:T(8,128)})) %all-reduce.3.cloned.1.call-update) | async-done | bytes 1769488 | tf_op jit(solution)/shard_map/psum | solution.py:67
  283.9 5.2 %fusion.2 = bf16[1,256,3072]{2,1,0:T(8,128)(2,1)} fusion(bf16[576,3072]{1,0:T(8,128)(2,1)} %reshape.202, f32[576]{0:T(1024)S(1)} %reshape.206, f32[576,256]{1,0:T(8,128)} %get-tuple-element.19, f32[576,256]{1,0:T(8,128)} %get-tuple-element.18), kind=kOutput, calls=%fused_computation.11 | convolution fusion | flops 907788288 | bytes 6293760 | tf_op jit(solution)/shard_map/dot_general | solution.py:72
  289.4 2.8 fusion
  292.8 6.4 %all-to-all-start.3 = ((f32[16,1,36]{2,1,0:T(1,128)}), f32[16,1,36]{2,1,0:T(1,128)S(1)}, u32[]{:S(2)}, u32[]{:S(2)}) async-start(f32[16,1,36]{2,1,0:T(1,128)} %all_to_all.19), calls=%async_computation.3 | async-start | bytes 16384 | tf_op jit(solution)/shard_map/all_to_all | solution.py:74
  299.2 4.7 %fusion.1 = bf16[1,256,3072]{2,1,0:T(8,128)(2,1)} fusion(bf16[576,3072]{1,0:T(8,128)(2,1)} %reshape.203, f32[576,256]{1,0:T(8,128)S(1)} %copy-done.5, f32[576]{0:T(1024)S(1)} %reshape.206, f32[576,256]{1,0:T(8,128)S(1)} %copy-done.4), kind=kOutput, calls=%fused_computation.10 | convolution fusion | flops 907788288 | bytes 6293760 | tf_op jit(solution)/shard_map/dot_general | solution.py:71
  305.1 2.3 gather_fusion.3
  (58 shorter events, 5.7 us)
Async XLA Ops:
  7.2 3.4 %copy-start = (bf16[256,3072]{1,0:T(8,128)(2,1)S(1)}, bf16[256,3072]{1,0:T(8,128)(2,1)}, u32[]{:S(2)}) copy-start(bf16[256,3072]{1,0:T(8,128)(2,1)} %param.7) | copy-start | bytes 4718596
  15.1 4.8 %copy-start.1 = (bf16[256,3072]{1,0:T(8,128)(2,1)S(1)}, bf16[256,3072]{1,0:T(8,128)(2,1)}, u32[]{:S(2)}) copy-start(bf16[256,3072]{1,0:T(8,128)(2,1)} %param.8) | copy-start | bytes 4718596
  126.2 91.1 %all-to-all-start.1 = ((bf16[16,36,3072]{2,1,0:T(8,128)(2,1)}), bf16[16,36,3072]{2,1,0:T(8,128)(2,1)}, u32[]{:S(2)}, u32[]{:S(2)}) async-start(bf16[16,36,3072]{2,1,0:T(8,128)(2,1)} %get-tuple-element.21), calls=%async_computation.1 | async-start | bytes 7864320 | tf_op jit(solution)/shard_map/all_to_all | solution.py:57
  132.6 4.9 %copy-start.9 = (bf16[1,256,3072]{2,1,0:T(8,128)(2,1)S(1)}, bf16[1,256,3072]{2,1,0:T(8,128)(2,1)}, u32[]{:S(2)}) copy-start(bf16[1,256,3072]{2,1,0:T(8,128)(2,1)} %param.11) | copy-start | bytes 4718596
  132.6 151.3 %all-reduce.3.cloned.1.call-start = ((), (), s32[]{:S(2)}) async-start(), calls=%async_computation.4 | async-start | bytes 3538944 | tf_op jit(solution)/shard_map/psum | solution.py:67
  137.4 4.1 %copy-start.2 = (bf16[576,3072]{1,0:T(8,128)(2,1)S(1)}, bf16[576,3072]{1,0:T(8,128)(2,1)}, u32[]{:S(2)}) copy-start(bf16[576,3072]{1,0:T(8,128)(2,1)} %reshape.203) | copy-start | bytes 10616836
  137.4 4.1 %copy-start.10 = (bf16[1,256,3072]{2,1,0:T(8,128)(2,1)S(1)}, bf16[1,256,3072]{2,1,0:T(8,128)(2,1)}, u32[]{:S(2)}) copy-start(bf16[1,256,3072]{2,1,0:T(8,128)(2,1)} %param.12) | copy-start | bytes 4718596
  143.5 78.5 %copy-start.11 = (bf16[1,256,3072]{2,1,0:T(8,128)(2,1)S(1)}, bf16[1,256,3072]{2,1,0:T(8,128)(2,1)}, u32[]{:S(2)}) copy-start(bf16[1,256,3072]{2,1,0:T(8,128)(2,1)} %param.13) | copy-start | bytes 4718596
  222.0 4.0 %copy-start.8 = (bf16[256,2]{0,1:T(2,128)(2,1)S(1)}, bf16[256,2]{0,1:T(2,128)(2,1)}, u32[]{:S(2)}) copy-start(bf16[256,2]{0,1:T(2,128)(2,1)} %param.9) | copy-start | bytes 3076
  226.0 12.0 %copy-start.7 = (s32[256,2]{0,1:T(2,128)S(1)}, s32[256,2]{0,1:T(2,128)}, u32[]{:S(2)}) copy-start(s32[256,2]{0,1:T(2,128)} %param.10) | copy-start | bytes 6148
  231.0 10.3 %all-to-all-start = ((bf16[16,1,36]{2,1,0:T(2,128)(2,1)}), bf16[16,1,36]{2,1,0:T(2,128)(2,1)S(1)}, u32[]{:S(2)}, u32[]{:S(2)}) async-start(bf16[16,1,36]{2,1,0:T(2,128)(2,1)} %select_n.80), calls=%async_computation | async-start | bytes 16384 | tf_op jit(solution)/shard_map/all_to_all | solution.py:58
  283.9 5.2 %copy-start.4 = (f32[576,256]{1,0:T(8,128)S(1)}, f32[576,256]{1,0:T(8,128)}, u32[]{:S(2)}) copy-start(f32[576,256]{1,0:T(8,128)} %get-tuple-element.18) | copy-start | bytes 1769476
  283.9 5.2 %copy-start.5 = (f32[576,256]{1,0:T(8,128)S(1)}, f32[576,256]{1,0:T(8,128)}, u32[]{:S(2)}) copy-start(f32[576,256]{1,0:T(8,128)} %get-tuple-element.20) | copy-start | bytes 1769476
  283.9 5.2 %copy-start.6 = (f32[576,256]{1,0:T(8,128)S(1)}, f32[576,256]{1,0:T(8,128)}, u32[]{:S(2)}) copy-start(f32[576,256]{1,0:T(8,128)} %get-tuple-element.19) | copy-start | bytes 1769476
  283.9 5.5 %copy-start.3 = (bf16[576,3072]{1,0:T(8,128)(2,1)S(1)}, bf16[576,3072]{1,0:T(8,128)(2,1)}, u32[]{:S(2)}) copy-start(bf16[576,3072]{1,0:T(8,128)(2,1)} %reshape.203) | copy-start | bytes 10616836
  292.8 11.0 %all-to-all-start.3 = ((f32[16,1,36]{2,1,0:T(1,128)}), f32[16,1,36]{2,1,0:T(1,128)S(1)}, u32[]{:S(2)}, u32[]{:S(2)}) async-start(f32[16,1,36]{2,1,0:T(1,128)} %all_to_all.19), calls=%async_computation.3 | async-start | bytes 16384 | tf_op jit(solution)/shard_map/all_to_all | solution.py:74
Sparse Core Ops, SparseCore 0:
  226.1 57.7 all-reduce.2
where the time goes:
time: 318 us; the launch traced here: 315 us
  waiting for transfers between devices  119 us (37%)
  blocking collectives  92 us (29%)
  local copies, waits for them, and re-layouts  39.4 us (12%)
  matrix products  22.6 us (7%)
  starting transfers between devices  19.8 us (6%)
  between operations  14.2 us (4%)
  other arithmetic  7.68 us (2%)
    all_to_all x1, blocking collectives, local(): lax.all_to_all(tok_slots, 'expert', split_axis=0, concat_axis=0, tiled=True)  92 us
    all_to_all x1, waiting for transfers between devices, local(): lax.all_to_all(grad_slots, 'expert', split_axis=0, concat_axis=0, tiled=T...  73.8 us
    psum x1, waiting for transfers between devices, local(): gate_sum, up_sum, grad_sum = lax.psum((gate_pre, up_pre, grad_hid), 'dp')  42.5 us
    gather x2, local copies, waits for them, and re-layouts, local(): tokens[token_of]  9.37 us
    gather x2, local copies, waits for them, and re-layouts, local(): grad_out[token_of]  9.33 us
    all_to_all x1, starting transfers between devices, local(): lax.all_to_all(prob_slots, 'expert', split_axis=0, concat_axis=0, tiled=T...  6.99 us
    all_to_all x1, starting transfers between devices, local(): lax.all_to_all(grad_slots, 'expert', split_axis=0, concat_axis=0, tiled=T...  6.4 us
  transfers between devices with their start and end apart: 4, of which 3 were waited for; matrix products, arithmetic and copies ran while one was open for 7% of the time, Pallas kernels for 0%

commit v1 on v0

v1 whole, which is shorter than its diff:
```python
import functools

import jax
import jax.numpy as jnp
from jax import lax
from jax.experimental import pallas as pl
from jax.experimental.pallas import tpu as pltpu
from jax.sharding import PartitionSpec as P

MESH = pl.DeviceIdType.MESH
F32 = jnp.float32
BF16 = jnp.bfloat16


def round_up(value, unit):
    return (value + unit - 1) // unit * unit


def partner_of(me, k, n):
    out, bit = 0, 1
    while bit < n:
        out = out + (me // bit + k // bit) % 2 * bit
        bit *= 2
    return out


def diagonal(rows):
    return lax.broadcasted_iota(jnp.int32, (rows, 128), 0) == lax.broadcasted_iota(
        jnp.int32, (rows, 128), 1
    )


def to_row(col):
    rows = col.shape[0]
    return jnp.sum(jnp.where(diagonal(rows), col, 0.0), axis=0, keepdims=True)


def to_col(row, rows):
    return jnp.sum(jnp.where(diagonal(rows), row, 0.0), axis=1, keepdims=True)


def kernel(
    n, dp, cap, groups,
    slots_ref, prob_ref, tok_ref, dy_ref, wg_ref, wu_ref, wd_ref,
    gate_ref, up_ref, down_ref, comb_ref,
    msg, recv, w_all, rows_a, acc, parts, p_out, p_in, s_out, s_in,
    w_sem, m_send, m_recv, p_send, p_recv, s_send, s_recv, y_send, y_recv,
):
    me = lax.axis_index("expert")
    mine = lax.axis_index("dp")
    tok_count, width = tok_ref.shape
    hid = wg_ref.shape[1]
    pair = msg.shape[1]
    rows = parts.shape[2]

    def w_copy(i):
        src = (wg_ref, wu_ref, wd_ref)[i]
        return pltpu.make_async_copy(src.at[0], w_all.at[pl.ds(i * hid, hid)], w_sem.at[i])

    for i in range(3):
        w_copy(i).start()

    barrier = pltpu.get_barrier_semaphore()

    def greet(k, _):
        pl.semaphore_signal(
            barrier, inc=1, device_id=(partner_of(me, k, n), mine), device_id_type=MESH
        )
        return 0

    lax.fori_loop(1, n, greet, 0)
    for j in range(1, dp):
        pl.semaphore_signal(
            barrier, inc=1, device_id=(me, (mine + j) % dp), device_id_type=MESH
        )
    pl.semaphore_wait(barrier, n - 1 + dp - 1)

    def msg_copy(k):
        return pltpu.make_async_remote_copy(
            src_ref=msg.at[k], dst_ref=recv.at[k], send_sem=m_send.at[k], recv_sem=m_recv.at[k],
            device_id=(partner_of(me, k, n), mine), device_id_type=MESH,
        )

    def p_copy(k):
        return pltpu.make_async_remote_copy(
            src_ref=p_out.at[k], dst_ref=p_in.at[k], send_sem=p_send.at[k], recv_sem=p_recv.at[k],
            device_id=(partner_of(me, k, n), mine), device_id_type=MESH,
        )

    def s_copy(k):
        return pltpu.make_async_remote_copy(
            src_ref=s_out.at[k], dst_ref=s_in.at[k], send_sem=s_send.at[k], recv_sem=s_recv.at[k],
            device_id=(partner_of(me, k, n), mine), device_id_type=MESH,
        )

    def y_copy(j, k):
        return pltpu.make_async_remote_copy(
            src_ref=parts.at[mine, k], dst_ref=parts.at[mine, k],
            send_sem=y_send.at[j, k], recv_sem=y_recv.at[mine, k],
            device_id=(me, (mine + j) % dp), device_id_type=MESH,
        )

    def y_arrival(j, k):
        other = (mine + j) % dp
        return pltpu.make_async_remote_copy(
            src_ref=parts.at[other, k], dst_ref=parts.at[other, k],
            send_sem=y_send.at[j, k], recv_sem=y_recv.at[other, k],
            device_id=(me, other), device_id_type=MESH,
        )

    def build(k, msg_to, p_to):
        dest = partner_of(me, k, n)
        place = lax.broadcasted_iota(jnp.int32, (pair, tok_count), 0)
        first = slots_ref[0:1, :] - dest * cap
        second = slots_ref[1:2, :] - dest * cap
        is_x = place < cap
        is_dy = (place >= cap) & (place < 2 * cap)
        pick_x = is_x & ((first == place) | (second == place))
        pick_dy = is_dy & ((first + cap == place) | (second + cap == place))
        picked = jnp.dot(
            jnp.where(pick_x, 1.0, 0.0).astype(BF16), tok_ref[...], preferred_element_type=F32
        ) + jnp.dot(
            jnp.where(pick_dy, 1.0, 0.0).astype(BF16), dy_ref[...], preferred_element_type=F32
        )
        msg_to[k] = picked.astype(BF16)
        spot = lax.broadcasted_iota(jnp.int32, (rows, tok_count), 0)
        prob = jnp.where(first == spot, prob_ref[0:1, :], 0.0) + jnp.where(
            second == spot, prob_ref[1:2, :], 0.0
        )
        p_to[k] = jnp.broadcast_to(
            to_row(jnp.sum(prob, axis=1, keepdims=True)), p_to.shape[1:]
        )

    half = n // 2

    def send(i, _):
        k = (half + i) % n + i // half
        build(k, msg, p_out)
        p_copy(k).start()
        msg_copy(k).start()
        return 0

    lax.fori_loop(0, n - 1, send, 0)
    build(0, recv, p_in)
    for i in range(3):
        w_copy(i).wait()

    def project(k):
        both = lax.dot_general(
            recv[k], w_all[...], (((1,), (1,)), ((), ())), preferred_element_type=F32
        )
        parts[mine, k, :, 0 : 2 * hid] = both[0:rows, 0 : 2 * hid]
        parts[mine, k, :, 2 * hid : 3 * hid] = pltpu.roll(
            both[:, 2 * hid : 3 * hid], pair - cap, 0
        )[0:rows]
        for j in range(1, dp):
            y_copy(j, k).start()

    def combine_rows(k):
        for j in range(1, dp):
            y_arrival(j, k).wait_recv()
        total = parts[0, k]
        for r in range(1, dp):
            total = total + parts[r, k]
        gate_pre = total[:, 0:hid]
        up_pre = total[:, hid : 2 * hid]
        grad_hid = total[:, 2 * hid : 3 * hid]
        real = lax.broadcasted_iota(jnp.int32, (rows, hid), 0) < cap
        weight = to_col(p_in[k][0:1, :], rows)
        sig = jax.nn.sigmoid(gate_pre)
        silu_out = gate_pre * sig
        slope = sig * (1.0 + gate_pre * (1.0 - sig))
        hidden = silu_out * up_pre
        scaled = weight * grad_hid
        scores = jnp.sum(jnp.where(real, hidden * grad_hid, 0.0), axis=1, keepdims=True)

        def spread(value):
            value = jnp.where(real, value, 0.0)
            return jnp.concatenate([value, jnp.zeros((pair - rows, hid), F32)], axis=0)

        rows_a[k, :, 0:hid] = spread(scaled * up_pre * slope).astype(BF16)
        rows_a[k, :, hid : 2 * hid] = spread(scaled * silu_out).astype(BF16)
        rows_a[k, :, 2 * hid : 3 * hid] = pltpu.roll(
            spread(weight * hidden), cap, 0
        ).astype(BF16)
        return jnp.broadcast_to(to_row(scores), s_out.shape[1:])

    def finish(k):
        s_out[k] = combine_rows(k)
        s_copy(k).start()

    def step(k, _):
        msg_copy(k).wait_recv()
        project(k)
        p_copy(k - 1).wait_recv()
        finish(k - 1)
        return 0

    tile = 512 if width % 512 == 0 else 256

    def outer(lo, hi, opening, closing):
        depth = (hi - lo) * pair

        def columns(c, _):
            at = pl.ds(pl.multiple_of(c * tile, tile), tile)
            new = lax.dot_general(
                rows_a[lo:hi].reshape(depth, 3 * hid), recv[lo:hi, :, at].reshape(depth, tile),
                (((0,), (0,)), ((), ())), preferred_element_type=F32,
            )
            if not opening:
                new = new + acc[:, at]
            if closing:
                gate_ref[0, :, at] = new[0:hid].astype(BF16)
                up_ref[0, :, at] = new[hid : 2 * hid].astype(BF16)
                down_ref[0, :, at] = new[2 * hid : 3 * hid].astype(BF16)
            else:
                acc[:, at] = new
            return 0

        lax.fori_loop(0, width // tile, columns, 0)

    project(0)
    msg_copy(1).wait_recv()
    project(1)
    s_in[0] = combine_rows(0)
    done = 0
    at = 2
    for g, bound in enumerate(groups):
        last = bound == n
        lax.fori_loop(at, min(bound + 1, n), step, 0)
        at = min(bound + 1, n)
        if last:
            p_copy(n - 1).wait_recv()
            finish(n - 1)
        outer(done, bound, g == 0, last)
        done = bound

    def gather_scores(k, carry):
        one, two = carry
        spot = lax.broadcasted_iota(jnp.int32, (rows, tok_count), 0)
        spot = jnp.where(spot < cap, spot + partner_of(me, k, n) * cap, -1)
        col = to_col(s_in[k][0:1, :], rows)
        one = one + jnp.sum(jnp.where(slots_ref[0:1, :] == spot, col, 0.0), axis=0, keepdims=True)
        two = two + jnp.sum(jnp.where(slots_ref[1:2, :] == spot, col, 0.0), axis=0, keepdims=True)
        return one, two

    def arrived(k, carry):
        s_copy(k).wait_recv()
        return gather_scores(k, carry)

    zero = jnp.zeros((1, tok_count), F32)
    one, two = lax.fori_loop(1, n, arrived, gather_scores(0, (zero, zero)))
    comb_ref[0:1, :] = one
    comb_ref[1:2, :] = two

    def drain(k, _):
        msg_copy(k).wait_send()
        p_copy(k).wait_send()
        s_copy(k).wait_send()
        return 0

    lax.fori_loop(1, n, drain, 0)

    def drain_parts(k, _):
        for j in range(1, dp):
            y_copy(j, k).wait_send()
        return 0

    lax.fori_loop(0, n, drain_parts, 0)


def local(n, dp, tokens, grad_out, combine, routes, w_gate, w_up, w_down):
    tok_count, width = tokens.shape
    hid = w_gate.shape[1]
    top_count = routes.shape[1]
    cap = max(2, (9 * tok_count * top_count + 8 * n - 1) // (8 * n))
    flat_expert = routes.reshape(-1)
    onehot = (flat_expert[:, None] == jnp.arange(n, dtype=jnp.int32)[None, :]).astype(jnp.int32)
    before = jnp.cumsum(onehot, axis=0) - onehot
    ranking = jnp.sum(before * onehot, axis=1)
    slot_of = (flat_expert * cap + ranking).reshape(tok_count, top_count).T
    probs = combine.astype(F32).T
    pair = round_up(2 * cap, 8)
    rows = round_up(cap, 8)
    groups = (n // 2, 3 * n // 4, n)
    grad_shape = jax.ShapeDtypeStruct((1, hid, width), BF16)
    vmem = pl.BlockSpec(memory_space=pltpu.VMEM)
    hbm = pl.BlockSpec(memory_space=pl.ANY)
    dma = pltpu.SemaphoreType.DMA
    gate, up, down, comb = pl.pallas_call(
        functools.partial(kernel, n, dp, cap, groups),
        out_shape=(
            grad_shape, grad_shape, grad_shape,
            jax.ShapeDtypeStruct((top_count, tok_count), F32),
        ),
        in_specs=[vmem] * 4 + [hbm] * 3,
        out_specs=(vmem,) * 4,
        scratch_shapes=[
            pltpu.VMEM((n, pair, width), BF16),
            pltpu.VMEM((n, pair, width), BF16),
            pltpu.VMEM((3 * hid, width), BF16),
            pltpu.VMEM((n, pair, 3 * hid), BF16),
            pltpu.VMEM((3 * hid, width), F32),
            pltpu.VMEM((dp, n, rows, 3 * hid), F32),
            pltpu.VMEM((n, 8, 128), F32),
            pltpu.VMEM((n, 8, 128), F32),
            pltpu.VMEM((n, 8, 128), F32),
            pltpu.VMEM((n, 8, 128), F32),
            dma((3,)),
            dma((n,)), dma((n,)), dma((n,)), dma((n,)), dma((n,)), dma((n,)),
            dma((dp, n)), dma((dp, n)),
        ],
        compiler_params=pltpu.CompilerParams(
            collective_id=0, has_side_effects=True, vmem_limit_bytes=60 * 1024 * 1024
        ),
        cost_estimate=pl.CostEstimate(
            flops=12 * n * cap * hid * width, bytes_accessed=20 * hid * width, transcendentals=0
        ),
    )(slot_of, probs, tokens, grad_out, w_gate, w_up, w_down)
    return gate, up, down, comb.T


def solution(mesh):
    placed = (
        P("expert", "dp"),
        P("expert", "dp"),
        P("expert", None),
        P("expert", None),
        P("expert", None, "dp"),
        P("expert", None, "dp"),
        P("expert", None, "dp"),
    )
    return jax.shard_map(
        functools.partial(local, mesh.shape["expert"], mesh.shape["dp"]),
        mesh=mesh,
        in_specs=placed,
        out_specs=(
            P("expert", None, "dp"),
            P("expert", None, "dp"),
            P("expert", None, "dp"),
            P("expert", None),
        ),
        check_vma=False,
    )
```

time: 318 us -> 196 us (0.62)
  the two profiles are of different devices: /device:TPU:19 before, /device:TPU:0 now
where the time goes in v1:
time: 196 us; the launch traced here: 195 us
  Pallas kernels  183 us (93%)
  local copies, waits for them, and re-layouts  8.01 us (4%)
  other arithmetic  3.83 us (2%)
    pallas_call x1, Pallas kernels, local(): pl.pallas_call(functools.partial(kernel, n, dp, cap, groups), out_shape=(...  183 us
    unnamed x11, local copies, waits for them, and re-layouts  7.28 us

profile of v1, /device:TPU:0, one launch (start us, length us, event | category | flops | bytes accessed | tf_op | source)
XLA Modules:
  0.0 195.4 jit_solution(1839728268423614977)
XLA Ops:
  0.6 1.3 convert_bitcast_fusion.prob_ref
  1.9 0.8 copy.11
  2.7 0.1 eq.29
  2.9 0.1 eq.25
  3.0 1.2 reduce-window.6
  4.2 0.2 slice_reduce_fusion
  4.4 0.1 fusion.2
  4.5 0.1 reduce_sum.12
  4.7 0.1 copy.14
  4.7 1.3 add_bitcast_fusion.1.slots_ref
  6.0 182.9 %shard_map.102 = (bf16[1,256,3072]{2,1,0:T(8,128)(2,1)}, bf16[1,256,3072]{2,1,0:T(8,128)(2,1)}, bf16[1,256,3072]{2,1,0:T(8,128)(2,1)}, f32[2,256]{1,0:T(2,128)}) custom-call(s32[2,256]{1,0:T(2,128)} %add_bitcast_fusion.1.slots_ref, f32[2,256]{1,0:T(2,128)} %convert_bitcast_fusion.prob_ref, bf16[256,3072]{1,0:T(8,128)(2,1)} %tok_ref.1, ...), custom_call_target="tpu_custom_call" | custom-call | flops 5435817984 | bytes 15728640 | tf_op jit(solution)/shard_map/pallas_call | solution.py:290
  188.9 0.0 copy-start.1
  188.9 2.8 %copy.21 = bf16[1,256,3072]{2,1,0:T(8,128)(2,1)} copy(bf16[1,256,3072]{2,1,0:T(8,128)(2,1)} %get-tuple-element.16) | data formatting | bytes 3145728
  191.7 0.0 copy-done.1
  191.7 0.0 copy-start
  191.7 1.1 copy.22
  192.8 0.8 copy-done
  193.7 0.0 copy-start.2
  193.7 1.1 copy.23
  194.8 0.0 copy-done.2
  194.8 0.6 copy.24
  (3 shorter events, 0.0 us)
Async XLA Ops:
  188.9 2.8 %copy-start.1 = (bf16[1,256,3072]{2,1,0:T(8,128)(2,1)S(1)}, bf16[1,256,3072]{2,1,0:T(8,128)(2,1)}, u32[]{:S(2)}) copy-start(bf16[1,256,3072]{2,1,0:T(8,128)(2,1)} %get-tuple-element.17) | copy-start | bytes 4718596
  191.7 2.0 %copy-start = (bf16[1,256,3072]{2,1,0:T(8,128)(2,1)S(1)}, bf16[1,256,3072]{2,1,0:T(8,128)(2,1)}, u32[]{:S(2)}) copy-start(bf16[1,256,3072]{2,1,0:T(8,128)(2,1)} %get-tuple-element.18) | copy-start | bytes 4718596
  193.7 1.1 copy-start.2

commit v2 on v1

--- a/solution.py
+++ b/solution.py
@@ -40,11 +40,11 @@
 
 
 def kernel(
-    n, dp, cap, groups,
-    slots_ref, prob_ref, tok_ref, dy_ref, wg_ref, wu_ref, wd_ref,
+    n, dp, cap, tile, ahead,
+    routes_ref, prob_ref, tok_ref, dy_ref, wg_ref, wu_ref, wd_ref,
     gate_ref, up_ref, down_ref, comb_ref,
-    msg, recv, w_all, rows_a, acc, parts, p_out, p_in, s_out, s_in,
-    w_sem, m_send, m_recv, p_send, p_recv, s_send, s_recv, y_send, y_recv,
+    slots_ref, msg, recv, staged, w_all, rows_a, acc, parts, p_out, p_in, s_out, s_in,
+    w_sem, m_send, m_recv, p_send, p_recv, s_send, s_recv, y_send, y_recv, o_sem,
 ):
     me = lax.axis_index("expert")
     mine = lax.axis_index("dp")
@@ -52,6 +52,13 @@
     hid = wg_ref.shape[1]
     pair = msg.shape[1]
     rows = parts.shape[2]
+    half = n // 2
+
+    def step_of(q):
+        return q % 2 * half + q // 2
+
+    def towards(q):
+        return (partner_of(me, step_of(q), n), mine)
 
     def w_copy(i):
         src = (wg_ref, wu_ref, wd_ref)[i]
@@ -75,22 +82,22 @@
         )
     pl.semaphore_wait(barrier, n - 1 + dp - 1)
 
-    def msg_copy(k):
+    def msg_copy(q):
         return pltpu.make_async_remote_copy(
-            src_ref=msg.at[k], dst_ref=recv.at[k], send_sem=m_send.at[k], recv_sem=m_recv.at[k],
-            device_id=(partner_of(me, k, n), mine), device_id_type=MESH,
-        )
-
-    def p_copy(k):
+            src_ref=msg.at[q], dst_ref=recv.at[q], send_sem=m_send.at[q], recv_sem=m_recv.at[q],
+            device_id=towards(q), device_id_type=MESH,
+        )
+
+    def p_copy(q):
         return pltpu.make_async_remote_copy(
-            src_ref=p_out.at[k], dst_ref=p_in.at[k], send_sem=p_send.at[k], recv_sem=p_recv.at[k],
-            device_id=(partner_of(me, k, n), mine), device_id_type=MESH,
-        )
-
-    def s_copy(k):
+            src_ref=p_out.at[q], dst_ref=p_in.at[q], send_sem=p_send.at[q], recv_sem=p_recv.at[q],
+            device_id=towards(q), device_id_type=MESH,
+        )
+
+    def s_copy(q):
         return pltpu.make_async_remote_copy(
-            src_ref=s_out.at[k], dst_ref=s_in.at[k], send_sem=s_send.at[k], recv_sem=s_recv.at[k],
-            device_id=(partner_of(me, k, n), mine), device_id_type=MESH,
+            src_ref=s_out.at[q], dst_ref=s_in.at[q], send_sem=s_send.at[q], recv_sem=s_recv.at[q],
+            device_id=towards(q), device_id_type=MESH,
         )
 
     def y_copy(j, k):
@@ -108,8 +115,22 @@
             device_id=(me, other), device_id_type=MESH,
         )
 
+    tokens_by = lax.broadcasted_iota(jnp.int32, (tok_count, tok_count), 0)
+    earlier = tokens_by < lax.broadcasted_iota(jnp.int32, (tok_count, tok_count), 1)
+    experts = lax.broadcasted_iota(jnp.int32, (round_up(n, 16), tok_count), 0)
+    named = [experts == routes_ref[j : j + 1, :] for j in range(2)]
+    before = jnp.dot(
+        jnp.where(named[0] | named[1], 1.0, 0.0).astype(BF16),
+        jnp.where(earlier, 1.0, 0.0).astype(BF16),
+        preferred_element_type=F32,
+    )
+    for j in range(2):
+        rank = jnp.sum(jnp.where(named[j], before, 0.0), axis=0, keepdims=True)
+        slots_ref[j : j + 1, :] = routes_ref[j : j + 1, :] * cap + rank.astype(jnp.int32)
+
     def build(k, msg_to, p_to):
-        dest = partner_of(me, k, n)
+        dest = towards(k)[0]
+        probs = prob_ref[...].astype(F32)
         place = lax.broadcasted_iota(jnp.int32, (pair, tok_count), 0)
         first = slots_ref[0:1, :] - dest * cap
         second = slots_ref[1:2, :] - dest * cap
@@ -124,23 +145,25 @@
         )
         msg_to[k] = picked.astype(BF16)
         spot = lax.broadcasted_iota(jnp.int32, (rows, tok_count), 0)
-        prob = jnp.where(first == spot, prob_ref[0:1, :], 0.0) + jnp.where(
-            second == spot, prob_ref[1:2, :], 0.0
+        prob = jnp.where(first == spot, probs[0:1, :], 0.0) + jnp.where(
+            second == spot, probs[1:2, :], 0.0
         )
         p_to[k] = jnp.broadcast_to(
             to_row(jnp.sum(prob, axis=1, keepdims=True)), p_to.shape[1:]
         )
 
-    half = n // 2
-
-    def send(i, _):
-        k = (half + i) % n + i // half
-        build(k, msg, p_out)
-        p_copy(k).start()
-        msg_copy(k).start()
-        return 0
-
-    lax.fori_loop(0, n - 1, send, 0)
+    def start(q):
+        p_copy(q).start()
+        msg_copy(q).start()
+
+    build(1, msg, p_out)
+    start(1)
+    for q in range(3, 2 * ahead, 2):
+        build(q, msg, p_out)
+        start(q)
+    for q in range(2, 2 * ahead, 2):
+        build(q, msg, p_out)
+        start(q)
     build(0, recv, p_in)
     for i in range(3):
         w_copy(i).wait()
@@ -185,18 +208,42 @@
         ).astype(BF16)
         return jnp.broadcast_to(to_row(scores), s_out.shape[1:])
 
-    def finish(k):
-        s_out[k] = combine_rows(k)
-        s_copy(k).start()
-
-    def step(k, _):
-        msg_copy(k).wait_recv()
-        project(k)
-        p_copy(k - 1).wait_recv()
-        finish(k - 1)
-        return 0
-
-    tile = 512 if width % 512 == 0 else 256
+    def finish(q):
+        p_copy(q).wait_recv()
+        s_out[q] = combine_rows(q)
+        s_copy(q).start()
+
+    def step(i, first=False):
+        near, far = 2 * i, 2 * i + 1
+        later = 2 * (i + ahead)
+        msg_copy(near).wait_recv()
+        project(near)
+        if first:
+            s_in[0] = combine_rows(0)
+        else:
+            finish(near - 2)
+        finish(far - 2)
+
+        @pl.when(i + ahead < half)
+        def _():
+            build(later + 1, msg, p_out)
+            build(later, msg, p_out)
+
+        msg_copy(far).wait_recv()
+
+        @pl.when(i + ahead < half)
+        def _():
+            msg_copy(far).wait_send()
+            start(later + 1)
+            start(later)
+
+        project(far)
+
+    def out_copy(j, c):
+        at = pl.ds(pl.multiple_of(c * tile, tile), tile)
+        return pltpu.make_async_copy(
+            staged.at[j, :, at], (gate_ref, up_ref, down_ref)[j].at[0, :, at], o_sem.at[j, c]
+        )
 
     def outer(lo, hi, opening, closing):
         depth = (hi - lo) * pair
@@ -210,9 +257,9 @@
             if not opening:
                 new = new + acc[:, at]
             if closing:
-                gate_ref[0, :, at] = new[0:hid].astype(BF16)
-                up_ref[0, :, at] = new[hid : 2 * hid].astype(BF16)
-                down_ref[0, :, at] = new[2 * hid : 3 * hid].astype(BF16)
+                for j in range(3):
+                    staged[j, :, at] = new[j * hid : (j + 1) * hid].astype(BF16)
+                    out_copy(j, c).start()
             else:
                 acc[:, at] = new
             return 0
@@ -220,25 +267,37 @@
         lax.fori_loop(0, width // tile, columns, 0)
 
     project(0)
+    build(2 * ahead + 1, msg, p_out)
+    build(2 * ahead, msg, p_out)
     msg_copy(1).wait_recv()
+    msg_copy(1).wait_send()
+    start(2 * ahead + 1)
+    start(2 * ahead)
     project(1)
-    s_in[0] = combine_rows(0)
-    done = 0
-    at = 2
-    for g, bound in enumerate(groups):
-        last = bound == n
-        lax.fori_loop(at, min(bound + 1, n), step, 0)
-        at = min(bound + 1, n)
-        if last:
-            p_copy(n - 1).wait_recv()
-            finish(n - 1)
-        outer(done, bound, g == 0, last)
-        done = bound
+    step(1, first=True)
+
+    def steps(i, _):
+        step(i)
+        return 0
+
+    lax.fori_loop(2, half // 2 + 1, steps, 0)
+    outer(0, half, True, False)
+    lax.fori_loop(half // 2 + 1, half - 1, steps, 0)
+    msg_copy(n - 2).wait_recv()
+    project(n - 2)
+    finish(n - 4)
+    outer(half, n - 3, False, False)
+    finish(n - 3)
+    msg_copy(n - 1).wait_recv()
+    project(n - 1)
+    finish(n - 2)
+    finish(n - 1)
+    outer(n - 3, n, False, True)
 
     def gather_scores(k, carry):
         one, two = carry
         spot = lax.broadcasted_iota(jnp.int32, (rows, tok_count), 0)
-        spot = jnp.where(spot < cap, spot + partner_of(me, k, n) * cap, -1)
+        spot = jnp.where(spot < cap, spot + towards(k)[0] * cap, -1)
         col = to_col(s_in[k][0:1, :], rows)
         one = one + jnp.sum(jnp.where(slots_ref[0:1, :] == spot, col, 0.0), axis=0, keepdims=True)
         two = two + jnp.sum(jnp.where(slots_ref[1:2, :] == spot, col, 0.0), axis=0, keepdims=True)
@@ -253,13 +312,19 @@
     comb_ref[0:1, :] = one
     comb_ref[1:2, :] = two
 
-    def drain(k, _):
-        msg_copy(k).wait_send()
-        p_copy(k).wait_send()
-        s_copy(k).wait_send()
+    def drain(q, _):
+        p_copy(q).wait_send()
+        s_copy(q).wait_send()
+        return 0
+
+    def drain_near(i, _):
+        msg_copy(2 * i).wait_send()
         return 0
 
     lax.fori_loop(1, n, drain, 0)
+    lax.fori_loop(1, half, drain_near, 0)
+    for i in range(half - ahead, half):
+        msg_copy(2 * i + 1).wait_send()
 
     def drain_parts(k, _):
         for j in range(1, dp):
@@ -267,6 +332,13 @@
         return 0
 
     lax.fori_loop(0, n, drain_parts, 0)
+
+    def drain_out(c, _):
+        for j in range(3):
+            out_copy(j, c).wait()
+        return 0
+
+    lax.fori_loop(0, width // tile, drain_out, 0)
 
 
 def local(n, dp, tokens, grad_out, combine, routes, w_gate, w_up, w_down):
@@ -274,30 +346,26 @@
     hid = w_gate.shape[1]
     top_count = routes.shape[1]
     cap = max(2, (9 * tok_count * top_count + 8 * n - 1) // (8 * n))
-    flat_expert = routes.reshape(-1)
-    onehot = (flat_expert[:, None] == jnp.arange(n, dtype=jnp.int32)[None, :]).astype(jnp.int32)
-    before = jnp.cumsum(onehot, axis=0) - onehot
-    ranking = jnp.sum(before * onehot, axis=1)
-    slot_of = (flat_expert * cap + ranking).reshape(tok_count, top_count).T
-    probs = combine.astype(F32).T
     pair = round_up(2 * cap, 8)
     rows = round_up(cap, 8)
-    groups = (n // 2, 3 * n // 4, n)
+    tile = 512 if width % 512 == 0 else 256
     grad_shape = jax.ShapeDtypeStruct((1, hid, width), BF16)
     vmem = pl.BlockSpec(memory_space=pltpu.VMEM)
     hbm = pl.BlockSpec(memory_space=pl.ANY)
     dma = pltpu.SemaphoreType.DMA
     gate, up, down, comb = pl.pallas_call(
-        functools.partial(kernel, n, dp, cap, groups),
+        functools.partial(kernel, n, dp, cap, tile, 2),
         out_shape=(
             grad_shape, grad_shape, grad_shape,
             jax.ShapeDtypeStruct((top_count, tok_count), F32),
         ),
         in_specs=[vmem] * 4 + [hbm] * 3,
-        out_specs=(vmem,) * 4,
+        out_specs=(hbm, hbm, hbm, vmem),
         scratch_shapes=[
+            pltpu.VMEM((top_count, tok_count), jnp.int32),
             pltpu.VMEM((n, pair, width), BF16),
             pltpu.VMEM((n, pair, width), BF16),
+            pltpu.VMEM((3, hid, width), BF16),
             pltpu.VMEM((3 * hid, width), BF16),
             pltpu.VMEM((n, pair, 3 * hid), BF16),
             pltpu.VMEM((3 * hid, width), F32),
@@ -308,7 +376,7 @@
             pltpu.VMEM((n, 8, 128), F32),
             dma((3,)),
             dma((n,)), dma((n,)), dma((n,)), dma((n,)), dma((n,)), dma((n,)),
-            dma((dp, n)), dma((dp, n)),
+            dma((dp, n)), dma((dp, n)), dma((3, width // tile)),
         ],
         compiler_params=pltpu.CompilerParams(
             collective_id=0, has_side_effects=True, vmem_limit_bytes=60 * 1024 * 1024
@@ -316,7 +384,7 @@
         cost_estimate=pl.CostEstimate(
             flops=12 * n * cap * hid * width, bytes_accessed=20 * hid * width, transcendentals=0
         ),
-    )(slot_of, probs, tokens, grad_out, w_gate, w_up, w_down)
+    )(routes.T, combine.T, tokens, grad_out, w_gate, w_up, w_down)
     return gate, up, down, comb.T
 
 

time: 196 us -> 196 us (level)
  the two profiles are of different devices: /device:TPU:0 before, /device:TPU:19 now
where the time goes in v2:
time: 196 us
  Pallas kernels  188 us (96%)
  local copies, waits for them, and re-layouts  6.47 us (3%)
    pallas_call x1, Pallas kernels, local(): pl.pallas_call(functools.partial(kernel, n, dp, cap, tile, 2), out_shape=...  188 us
    unnamed x10, local copies, waits for them, and re-layouts  6.47 us

profile of v2, /device:TPU:19, one launch (start us, length us, event | category | flops | bytes accessed | tf_op | source)
XLA Modules:
  0.0 195.5 jit_solution(2169073352752534471)
XLA Ops:
  0.6 188.4 %shard_map.102 = (bf16[1,256,3072]{2,1,0:T(8,128)(2,1)}, bf16[1,256,3072]{2,1,0:T(8,128)(2,1)}, bf16[1,256,3072]{2,1,0:T(8,128)(2,1)}, f32[2,256]{1,0:T(2,128)}) custom-call(s32[2,256]{1,0:T(2,128)} %bitcast.4, bf16[2,256]{1,0:T(2,128)(2,1)} %bitcast.5, bf16[256,3072]{1,0:T(8,128)(2,1)} %tok_ref.1, bf16[256,3072]{1,0:T(8,128)(2,1)} %dy_ref.1, ...), custom_call_target="tpu_custom_call" | custom-call | flops 5435817984 | bytes 15728640 | tf_op jit(solution)/shard_map/pallas_call | solution.py:356
  189.0 0.0 copy-start.1
  189.0 2.8 %copy.15 = bf16[1,256,3072]{2,1,0:T(8,128)(2,1)} copy(bf16[1,256,3072]{2,1,0:T(8,128)(2,1)} %get-tuple-element.16) | data formatting | bytes 3145728
  191.8 0.0 copy-done.1
  191.8 0.0 copy-start
  191.8 1.1 copy.16
  193.0 0.8 copy-done
  193.8 0.0 copy-start.2
  193.8 1.1 copy.17
  194.9 0.0 copy-done.2
  194.9 0.6 copy.18
Async XLA Ops:
  189.0 2.8 %copy-start.1 = (bf16[1,256,3072]{2,1,0:T(8,128)(2,1)S(1)}, bf16[1,256,3072]{2,1,0:T(8,128)(2,1)}, u32[]{:S(2)}) copy-start(bf16[1,256,3072]{2,1,0:T(8,128)(2,1)} %get-tuple-element.17) | copy-start | bytes 4718596
  191.8 2.0 %copy-start = (bf16[1,256,3072]{2,1,0:T(8,128)(2,1)S(1)}, bf16[1,256,3072]{2,1,0:T(8,128)(2,1)}, u32[]{:S(2)}) copy-start(bf16[1,256,3072]{2,1,0:T(8,128)(2,1)} %get-tuple-element.18) | copy-start | bytes 4718596
  193.8 1.1 copy-start.2

commit v3 on v2

--- a/solution.py
+++ b/solution.py
@@ -40,7 +40,7 @@
 
 
 def kernel(
-    n, dp, cap, tile, ahead,
+    n, dp, cap, tile, groups,
     routes_ref, prob_ref, tok_ref, dy_ref, wg_ref, wu_ref, wd_ref,
     gate_ref, up_ref, down_ref, comb_ref,
     slots_ref, msg, recv, staged, w_all, rows_a, acc, parts, p_out, p_in, s_out, s_in,
@@ -54,15 +54,12 @@
     rows = parts.shape[2]
     half = n // 2
 
-    def step_of(q):
-        return q % 2 * half + q // 2
-
-    def towards(q):
-        return (partner_of(me, step_of(q), n), mine)
+    def towards(k):
+        return (partner_of(me, k, n), mine)
 
     def w_copy(i):
         src = (wg_ref, wu_ref, wd_ref)[i]
-        return pltpu.make_async_copy(src.at[0], w_all.at[pl.ds(i * hid, hid)], w_sem.at[i])
+        return pltpu.make_async_copy(src.at[0], staged.at[i], w_sem.at[i])
 
     for i in range(3):
         w_copy(i).start()
@@ -156,21 +153,28 @@
         p_copy(q).start()
         msg_copy(q).start()
 
-    build(1, msg, p_out)
-    start(1)
-    for q in range(3, 2 * ahead, 2):
-        build(q, msg, p_out)
-        start(q)
-    for q in range(2, 2 * ahead, 2):
-        build(q, msg, p_out)
-        start(q)
+    def send(i, _):
+        k = (half + i) % n + i // half
+        build(k, msg, p_out)
+        start(k)
+        return 0
+
+    lax.fori_loop(0, n - 1, send, 0)
     build(0, recv, p_in)
     for i in range(3):
         w_copy(i).wait()
 
+    def turn(c, _):
+        at = pl.ds(pl.multiple_of(c * tile, tile), tile)
+        for i in range(3):
+            w_all[at, i * hid : (i + 1) * hid] = staged[i, :, at].T
+        return 0
+
+    lax.fori_loop(0, width // tile, turn, 0)
+
     def project(k):
         both = lax.dot_general(
-            recv[k], w_all[...], (((1,), (1,)), ((), ())), preferred_element_type=F32
+            recv[k], w_all[...], (((1,), (0,)), ((), ())), preferred_element_type=F32
         )
         parts[mine, k, :, 0 : 2 * hid] = both[0:rows, 0 : 2 * hid]
         parts[mine, k, :, 2 * hid : 3 * hid] = pltpu.roll(
@@ -213,31 +217,11 @@
         s_out[q] = combine_rows(q)
         s_copy(q).start()
 
-    def step(i, first=False):
-        near, far = 2 * i, 2 * i + 1
-        later = 2 * (i + ahead)
-        msg_copy(near).wait_recv()
-        project(near)
-        if first:
-            s_in[0] = combine_rows(0)
-        else:
-            finish(near - 2)
-        finish(far - 2)
-
-        @pl.when(i + ahead < half)
-        def _():
-            build(later + 1, msg, p_out)
-            build(later, msg, p_out)
-
-        msg_copy(far).wait_recv()
-
-        @pl.when(i + ahead < half)
-        def _():
-            msg_copy(far).wait_send()
-            start(later + 1)
-            start(later)
-
-        project(far)
+    def step(k, _):
+        msg_copy(k).wait_recv()
+        project(k)
+        finish(k - 1)
+        return 0
 
     def out_copy(j, c):
         at = pl.ds(pl.multiple_of(c * tile, tile), tile)
@@ -247,12 +231,12 @@
 
     def outer(lo, hi, opening, closing):
         depth = (hi - lo) * pair
+        turned = rows_a[lo:hi].reshape(depth, 3 * hid).T
 
         def columns(c, _):
             at = pl.ds(pl.multiple_of(c * tile, tile), tile)
-            new = lax.dot_general(
-                rows_a[lo:hi].reshape(depth, 3 * hid), recv[lo:hi, :, at].reshape(depth, tile),
-                (((0,), (0,)), ((), ())), preferred_element_type=F32,
+            new = jnp.dot(
+                turned, recv[lo:hi, :, at].reshape(depth, tile), preferred_element_type=F32
             )
             if not opening:
                 new = new + acc[:, at]
@@ -267,32 +251,17 @@
         lax.fori_loop(0, width // tile, columns, 0)
 
     project(0)
-    build(2 * ahead + 1, msg, p_out)
-    build(2 * ahead, msg, p_out)
     msg_copy(1).wait_recv()
-    msg_copy(1).wait_send()
-    start(2 * ahead + 1)
-    start(2 * ahead)
     project(1)
-    step(1, first=True)
-
-    def steps(i, _):
-        step(i)
-        return 0
-
-    lax.fori_loop(2, half // 2 + 1, steps, 0)
-    outer(0, half, True, False)
-    lax.fori_loop(half // 2 + 1, half - 1, steps, 0)
-    msg_copy(n - 2).wait_recv()
-    project(n - 2)
-    finish(n - 4)
-    outer(half, n - 3, False, False)
-    finish(n - 3)
-    msg_copy(n - 1).wait_recv()
-    project(n - 1)
-    finish(n - 2)
-    finish(n - 1)
-    outer(n - 3, n, False, True)
+    s_in[0] = combine_rows(0)
+    done, k = 0, 2
+    for bound in groups:
+        lax.fori_loop(k, min(bound + 1, n), step, 0)
+        k = min(bound + 1, n)
+        if bound == n:
+            finish(n - 1)
+        outer(done, bound, done == 0, bound == n)
+        done = bound
 
     def gather_scores(k, carry):
         one, two = carry
@@ -312,19 +281,13 @@
     comb_ref[0:1, :] = one
     comb_ref[1:2, :] = two
 
-    def drain(q, _):
-        p_copy(q).wait_send()
-        s_copy(q).wait_send()
-        return 0
-
-    def drain_near(i, _):
-        msg_copy(2 * i).wait_send()
+    def drain(k, _):
+        msg_copy(k).wait_send()
+        p_copy(k).wait_send()
+        s_copy(k).wait_send()
         return 0
 
     lax.fori_loop(1, n, drain, 0)
-    lax.fori_loop(1, half, drain_near, 0)
-    for i in range(half - ahead, half):
-        msg_copy(2 * i + 1).wait_send()
 
     def drain_parts(k, _):
         for j in range(1, dp):
@@ -354,7 +317,7 @@
     hbm = pl.BlockSpec(memory_space=pl.ANY)
     dma = pltpu.SemaphoreType.DMA
     gate, up, down, comb = pl.pallas_call(
-        functools.partial(kernel, n, dp, cap, tile, 2),
+        functools.partial(kernel, n, dp, cap, tile, (n // 2, n - 3, n)),
         out_shape=(
             grad_shape, grad_shape, grad_shape,
             jax.ShapeDtypeStruct((top_count, tok_count), F32),
@@ -366,7 +329,7 @@
             pltpu.VMEM((n, pair, width), BF16),
             pltpu.VMEM((n, pair, width), BF16),
             pltpu.VMEM((3, hid, width), BF16),
-            pltpu.VMEM((3 * hid, width), BF16),
+            pltpu.VMEM((width, 3 * hid), BF16),
             pltpu.VMEM((n, pair, 3 * hid), BF16),
             pltpu.VMEM((3 * hid, width), F32),
             pltpu.VMEM((dp, n, rows, 3 * hid), F32),
@@ -379,7 +342,7 @@
             dma((dp, n)), dma((dp, n)), dma((3, width // tile)),
         ],
         compiler_params=pltpu.CompilerParams(
-            collective_id=0, has_side_effects=True, vmem_limit_bytes=60 * 1024 * 1024
+            collective_id=0, has_side_effects=True, vmem_limit_bytes=47 * 1024 * 1024
         ),
         cost_estimate=pl.CostEstimate(
             flops=12 * n * cap * hid * width, bytes_accessed=20 * hid * width, transcendentals=0

time: 196 us -> 182 us (0.929)
  Pallas kernels: 188 us -> 174 us
    pallas_call x1, Pallas kernels: 188 us -> 174 us  [local(): pl.pallas_call(functools.partial(kernel, n, dp, cap, tile, (n // 2, n - 3...]
where the time goes in v3:
time: 182 us; the launch traced here: 181 us
  Pallas kernels  174 us (96%)
  local copies, waits for them, and re-layouts  6.77 us (4%)
    pallas_call x1, Pallas kernels, local(): pl.pallas_call(functools.partial(kernel, n, dp, cap, tile, (n // 2, n - 3...  174 us
    unnamed x10, local copies, waits for them, and re-layouts  6.77 us

profile of v3, /device:TPU:19, one launch (start us, length us, event | category | flops | bytes accessed | tf_op | source)
XLA Modules:
  0.0 181.1 jit_solution(11434471559036101750)
XLA Ops:
  0.6 0.0 copy-start
  0.6 1.4 copy-done
  2.0 0.0 copy-start.1
  2.0 0.7 copy-done.1
  2.7 0.0 copy-start.2
  2.7 0.7 copy-done.2
  3.4 173.7 %shard_map.102 = (bf16[1,256,3072]{2,1,0:T(8,128)(2,1)S(1)}, bf16[1,256,3072]{2,1,0:T(8,128)(2,1)S(1)}, bf16[1,256,3072]{2,1,0:T(8,128)(2,1)S(1)}, f32[2,256]{1,0:T(2,128)S(1)}) custom-call(s32[2,256]{1,0:T(2,128)S(1)} %bitcast.4, bf16[2,256]{1,0:T(2,128)(2,1)S(1)} %bitcast.5, bf16[256,3072]{1,0:T(8,128)(2,1)S(1)} %copy-done, bf16[256,3072]{1,0:T(8,128)(2,1)} %dy_ref.1, ...), custom_call_target="tpu_custom_call" | custom-call | flops 5435817984 | bytes 15728640 | tf_op jit(solution)/shard_map/pallas_call | solution.py:319
  177.1 1.1 copy.15
  178.3 1.1 copy.16
  179.4 1.1 copy.17
  180.6 0.6 copy.18
Async XLA Ops:
  0.6 1.4 copy-start
  2.0 0.7 copy-start.1
  2.7 0.7 copy-start.2

commit v4 on v3

--- a/solution.py
+++ b/solution.py
@@ -51,7 +51,7 @@
     tok_count, width = tok_ref.shape
     hid = wg_ref.shape[1]
     pair = msg.shape[1]
-    rows = parts.shape[2]
+    rows = parts.shape[2] // 2
     half = n // 2
 
     def towards(k):
@@ -172,55 +172,69 @@
 
     lax.fori_loop(0, width // tile, turn, 0)
 
-    def project(k):
-        both = lax.dot_general(
-            recv[k], w_all[...], (((1,), (0,)), ((), ())), preferred_element_type=F32
-        )
-        parts[mine, k, :, 0 : 2 * hid] = both[0:rows, 0 : 2 * hid]
-        parts[mine, k, :, 2 * hid : 3 * hid] = pltpu.roll(
-            both[:, 2 * hid : 3 * hid], pair - cap, 0
-        )[0:rows]
-        for j in range(1, dp):
-            y_copy(j, k).start()
-
-    def combine_rows(k):
-        for j in range(1, dp):
-            y_arrival(j, k).wait_recv()
-        total = parts[0, k]
+    def project(j):
+        both = jnp.dot(
+            recv[pl.ds(2 * j, 2)].reshape(2 * pair, width), w_all[...], preferred_element_type=F32
+        )
+        held = []
+        for b in range(2):
+            block = both[b * pair : (b + 1) * pair]
+            moved = pltpu.roll(block[:, 2 * hid : 3 * hid], pair - cap, 0)
+            held.append(jnp.concatenate([block[0:rows, 0 : 2 * hid], moved[0:rows]], axis=1))
+        parts[mine, j] = jnp.concatenate(held, axis=0).astype(BF16)
+        for other in range(1, dp):
+            y_copy(other, j).start()
+
+    def combine_rows(j):
+        for other in range(1, dp):
+            y_arrival(other, j).wait_recv()
+        total = parts[0, j].astype(F32)
         for r in range(1, dp):
-            total = total + parts[r, k]
+            total = total + parts[r, j].astype(F32)
         gate_pre = total[:, 0:hid]
         up_pre = total[:, hid : 2 * hid]
         grad_hid = total[:, 2 * hid : 3 * hid]
         real = lax.broadcasted_iota(jnp.int32, (rows, hid), 0) < cap
-        weight = to_col(p_in[k][0:1, :], rows)
+        weight = jnp.concatenate(
+            [to_col(p_in[2 * j][0:1, :], rows), to_col(p_in[2 * j + 1][0:1, :], rows)], axis=0
+        )
         sig = jax.nn.sigmoid(gate_pre)
         silu_out = gate_pre * sig
         slope = sig * (1.0 + gate_pre * (1.0 - sig))
         hidden = silu_out * up_pre
         scaled = weight * grad_hid
-        scores = jnp.sum(jnp.where(real, hidden * grad_hid, 0.0), axis=1, keepdims=True)
-
-        def spread(value):
-            value = jnp.where(real, value, 0.0)
-            return jnp.concatenate([value, jnp.zeros((pair - rows, hid), F32)], axis=0)
-
-        rows_a[k, :, 0:hid] = spread(scaled * up_pre * slope).astype(BF16)
-        rows_a[k, :, hid : 2 * hid] = spread(scaled * silu_out).astype(BF16)
-        rows_a[k, :, 2 * hid : 3 * hid] = pltpu.roll(
-            spread(weight * hidden), cap, 0
-        ).astype(BF16)
-        return jnp.broadcast_to(to_row(scores), s_out.shape[1:])
-
-    def finish(q):
-        p_copy(q).wait_recv()
-        s_out[q] = combine_rows(q)
-        s_copy(q).start()
-
-    def step(k, _):
-        msg_copy(k).wait_recv()
-        project(k)
-        finish(k - 1)
+        products = hidden * grad_hid
+        scores = []
+        for b in range(2):
+            here = slice(b * rows, (b + 1) * rows)
+
+            def spread(value):
+                value = jnp.where(real, value[here], 0.0)
+                return jnp.concatenate([value, jnp.zeros((pair - rows, hid), F32)], axis=0)
+
+            k = 2 * j + b
+            rows_a[k, :, 0:hid] = spread(scaled * up_pre * slope).astype(BF16)
+            rows_a[k, :, hid : 2 * hid] = spread(scaled * silu_out).astype(BF16)
+            rows_a[k, :, 2 * hid : 3 * hid] = pltpu.roll(
+                spread(weight * hidden), cap, 0
+            ).astype(BF16)
+            col = jnp.sum(jnp.where(real, products[here], 0.0), axis=1, keepdims=True)
+            scores.append(jnp.broadcast_to(to_row(col), s_out.shape[1:]))
+        return scores
+
+    def finish(j):
+        p_copy(2 * j).wait_recv()
+        p_copy(2 * j + 1).wait_recv()
+        scores = combine_rows(j)
+        for b in range(2):
+            s_out[2 * j + b] = scores[b]
+            s_copy(2 * j + b).start()
+
+    def step(j, _):
+        msg_copy(2 * j).wait_recv()
+        msg_copy(2 * j + 1).wait_recv()
+        project(j)
+        finish(j - 1)
         return 0
 
     def out_copy(j, c):
@@ -250,16 +264,23 @@
 
         lax.fori_loop(0, width // tile, columns, 0)
 
+    msg_copy(1).wait_recv()
     project(0)
-    msg_copy(1).wait_recv()
+    msg_copy(2).wait_recv()
+    msg_copy(3).wait_recv()
     project(1)
-    s_in[0] = combine_rows(0)
-    done, k = 0, 2
+    p_copy(1).wait_recv()
+    scores = combine_rows(0)
+    s_in[0] = scores[0]
+    s_out[1] = scores[1]
+    s_copy(1).start()
+    done, j = 0, 2
     for bound in groups:
-        lax.fori_loop(k, min(bound + 1, n), step, 0)
-        k = min(bound + 1, n)
+        upto = min(bound // 2 + 1, half)
+        lax.fori_loop(j, upto, step, 0)
+        j = upto
         if bound == n:
-            finish(n - 1)
+            finish(half - 1)
         outer(done, bound, done == 0, bound == n)
         done = bound
 
@@ -289,12 +310,12 @@
 
     lax.fori_loop(1, n, drain, 0)
 
-    def drain_parts(k, _):
-        for j in range(1, dp):
-            y_copy(j, k).wait_send()
-        return 0
-
-    lax.fori_loop(0, n, drain_parts, 0)
+    def drain_parts(j, _):
+        for other in range(1, dp):
+            y_copy(other, j).wait_send()
+        return 0
+
+    lax.fori_loop(0, half, drain_parts, 0)
 
     def drain_out(c, _):
         for j in range(3):
@@ -317,7 +338,7 @@
     hbm = pl.BlockSpec(memory_space=pl.ANY)
     dma = pltpu.SemaphoreType.DMA
     gate, up, down, comb = pl.pallas_call(
-        functools.partial(kernel, n, dp, cap, tile, (n // 2, n - 3, n)),
+        functools.partial(kernel, n, dp, cap, tile, (n // 2, n - 2, n)),
         out_shape=(
             grad_shape, grad_shape, grad_shape,
             jax.ShapeDtypeStruct((top_count, tok_count), F32),
@@ -332,14 +353,14 @@
             pltpu.VMEM((width, 3 * hid), BF16),
             pltpu.VMEM((n, pair, 3 * hid), BF16),
             pltpu.VMEM((3 * hid, width), F32),
-            pltpu.VMEM((dp, n, rows, 3 * hid), F32),
+            pltpu.VMEM((dp, n // 2, 2 * rows, 3 * hid), BF16),
             pltpu.VMEM((n, 8, 128), F32),
             pltpu.VMEM((n, 8, 128), F32),
             pltpu.VMEM((n, 8, 128), F32),
             pltpu.VMEM((n, 8, 128), F32),
             dma((3,)),
             dma((n,)), dma((n,)), dma((n,)), dma((n,)), dma((n,)), dma((n,)),
-            dma((dp, n)), dma((dp, n)), dma((3, width // tile)),
+            dma((dp, n // 2)), dma((dp, n // 2)), dma((3, width // tile)),
         ],
         compiler_params=pltpu.CompilerParams(
             collective_id=0, has_side_effects=True, vmem_limit_bytes=47 * 1024 * 1024

time: 182 us -> 181 us (level)
  no operation moved by 1% of the time
where the time goes in v4:
time: 181 us
  Pallas kernels  173 us (96%)
  local copies, waits for them, and re-layouts  6.77 us (4%)
    pallas_call x1, Pallas kernels, local(): pl.pallas_call(functools.partial(kernel, n, dp, cap, tile, (n // 2, n - 2...  173 us
    unnamed x10, local copies, waits for them, and re-layouts  6.77 us

profile of v4, /device:TPU:19, one launch (start us, length us, event | category | flops | bytes accessed | tf_op | source)
XLA Modules:
  0.0 180.7 jit_solution(17117795715551339141)
XLA Ops:
  0.6 0.0 copy-start
  0.6 1.4 copy-done
  2.0 0.0 copy-start.1
  2.0 0.7 copy-done.1
  2.7 0.0 copy-start.2
  2.7 0.7 copy-done.2
  3.4 173.3 %shard_map.102 = (bf16[1,256,3072]{2,1,0:T(8,128)(2,1)S(1)}, bf16[1,256,3072]{2,1,0:T(8,128)(2,1)S(1)}, bf16[1,256,3072]{2,1,0:T(8,128)(2,1)S(1)}, f32[2,256]{1,0:T(2,128)S(1)}) custom-call(s32[2,256]{1,0:T(2,128)S(1)} %bitcast.4, bf16[2,256]{1,0:T(2,128)(2,1)S(1)} %bitcast.5, bf16[256,3072]{1,0:T(8,128)(2,1)S(1)} %copy-done, bf16[256,3072]{1,0:T(8,128)(2,1)} %dy_ref.1, ...), custom_call_target="tpu_custom_call" | custom-call | flops 5435817984 | bytes 15728640 | tf_op jit(solution)/shard_map/pallas_call | solution.py:340
  176.7 1.1 copy.15
  177.9 1.1 copy.16
  179.0 1.1 copy.17
  180.2 0.6 copy.18
Async XLA Ops:
  0.6 1.4 copy-start
  2.0 0.7 copy-start.1
  2.7 0.7 copy-start.2

commit v5 on v4

--- a/solution.py
+++ b/solution.py
@@ -55,7 +55,7 @@
     half = n // 2
 
     def towards(k):
-        return (partner_of(me, k, n), mine)
+        return (partner_of(me, k % 2 * half + k // 2, n), mine)
 
     def w_copy(i):
         src = (wg_ref, wu_ref, wd_ref)[i]
@@ -154,12 +154,14 @@
         msg_copy(q).start()
 
     def send(i, _):
-        k = (half + i) % n + i // half
+        k = i + i % 2 * 2
         build(k, msg, p_out)
         start(k)
         return 0
 
-    lax.fori_loop(0, n - 1, send, 0)
+    build(1, msg, p_out)
+    start(1)
+    lax.fori_loop(1, n - 1, send, 0)
     build(0, recv, p_in)
     for i in range(3):
         w_copy(i).wait()
@@ -181,16 +183,16 @@
             block = both[b * pair : (b + 1) * pair]
             moved = pltpu.roll(block[:, 2 * hid : 3 * hid], pair - cap, 0)
             held.append(jnp.concatenate([block[0:rows, 0 : 2 * hid], moved[0:rows]], axis=1))
-        parts[mine, j] = jnp.concatenate(held, axis=0).astype(BF16)
+        parts[mine, j] = jnp.concatenate(held, axis=0)
         for other in range(1, dp):
             y_copy(other, j).start()
 
     def combine_rows(j):
         for other in range(1, dp):
             y_arrival(other, j).wait_recv()
-        total = parts[0, j].astype(F32)
+        total = parts[0, j]
         for r in range(1, dp):
-            total = total + parts[r, j].astype(F32)
+            total = total + parts[r, j]
         gate_pre = total[:, 0:hid]
         up_pre = total[:, hid : 2 * hid]
         grad_hid = total[:, 2 * hid : 3 * hid]
@@ -353,7 +355,7 @@
             pltpu.VMEM((width, 3 * hid), BF16),
             pltpu.VMEM((n, pair, 3 * hid), BF16),
             pltpu.VMEM((3 * hid, width), F32),
-            pltpu.VMEM((dp, n // 2, 2 * rows, 3 * hid), BF16),
+            pltpu.VMEM((dp, n // 2, 2 * rows, 3 * hid), F32),
             pltpu.VMEM((n, 8, 128), F32),
             pltpu.VMEM((n, 8, 128), F32),
             pltpu.VMEM((n, 8, 128), F32),

time: 181 us -> 184 us (1.017)
  Pallas kernels: 173 us -> 176 us
    pallas_call x1, Pallas kernels: 173 us -> 176 us  [local(): pl.pallas_call(functools.partial(kernel, n, dp, cap, tile, (n // 2, n - 2...]
where the time goes in v5:
time: 184 us
  Pallas kernels  176 us (96%)
  local copies, waits for them, and re-layouts  6.77 us (4%)
    pallas_call x1, Pallas kernels, local(): pl.pallas_call(functools.partial(kernel, n, dp, cap, tile, (n // 2, n - 2...  176 us
    unnamed x10, local copies, waits for them, and re-layouts  6.77 us

profile of v5, /device:TPU:19, one launch (start us, length us, event | category | flops | bytes accessed | tf_op | source)
XLA Modules:
  0.0 183.6 jit_solution(9116542528894339309)
XLA Ops:
  0.6 0.0 copy-start
  0.6 1.4 copy-done
  2.0 0.0 copy-start.1
  2.0 0.7 copy-done.1
  2.7 0.0 copy-start.2
  2.7 0.7 copy-done.2
  3.4 176.2 %shard_map.102 = (bf16[1,256,3072]{2,1,0:T(8,128)(2,1)S(1)}, bf16[1,256,3072]{2,1,0:T(8,128)(2,1)S(1)}, bf16[1,256,3072]{2,1,0:T(8,128)(2,1)S(1)}, f32[2,256]{1,0:T(2,128)S(1)}) custom-call(s32[2,256]{1,0:T(2,128)S(1)} %bitcast.4, bf16[2,256]{1,0:T(2,128)(2,1)S(1)} %bitcast.5, bf16[256,3072]{1,0:T(8,128)(2,1)S(1)} %copy-done, bf16[256,3072]{1,0:T(8,128)(2,1)} %dy_ref.1, ...), custom_call_target="tpu_custom_call" | custom-call | flops 5435817984 | bytes 15728640 | tf_op jit(solution)/shard_map/pallas_call | solution.py:342
  179.6 1.1 copy.15
  180.8 1.1 copy.16
  181.9 1.1 copy.17
  183.0 0.6 copy.18
Async XLA Ops:
  0.6 1.4 copy-start
  2.0 0.7 copy-start.1
  2.7 0.7 copy-start.2

commit v6 on v5

--- a/solution.py
+++ b/solution.py
@@ -55,7 +55,7 @@
     half = n // 2
 
     def towards(k):
-        return (partner_of(me, k % 2 * half + k // 2, n), mine)
+        return (partner_of(me, k, n), mine)
 
     def w_copy(i):
         src = (wg_ref, wu_ref, wd_ref)[i]
@@ -154,14 +154,12 @@
         msg_copy(q).start()
 
     def send(i, _):
-        k = i + i % 2 * 2
+        k = (half + i) % n + i // half
         build(k, msg, p_out)
         start(k)
         return 0
 
-    build(1, msg, p_out)
-    start(1)
-    lax.fori_loop(1, n - 1, send, 0)
+    lax.fori_loop(0, n - 1, send, 0)
     build(0, recv, p_in)
     for i in range(3):
         w_copy(i).wait()

time: 184 us -> 184 us (level)
  no operation moved by 1% of the time
where the time goes in v6:
time: 184 us; the launch traced here: 183 us
  Pallas kernels  176 us (96%)
  local copies, waits for them, and re-layouts  6.77 us (4%)
    pallas_call x1, Pallas kernels, local(): pl.pallas_call(functools.partial(kernel, n, dp, cap, tile, (n // 2, n - 2...  176 us
    unnamed x10, local copies, waits for them, and re-layouts  6.77 us

profile of v6, /device:TPU:19, one launch (start us, length us, event | category | flops | bytes accessed | tf_op | source)
XLA Modules:
  0.0 183.2 jit_solution(4763099131914348597)
XLA Ops:
  0.6 0.0 copy-start
  0.6 1.4 copy-done
  2.0 0.0 copy-start.1
  2.0 0.7 copy-done.1
  2.7 0.0 copy-start.2
  2.7 0.7 copy-done.2
  3.4 175.8 %shard_map.102 = (bf16[1,256,3072]{2,1,0:T(8,128)(2,1)S(1)}, bf16[1,256,3072]{2,1,0:T(8,128)(2,1)S(1)}, bf16[1,256,3072]{2,1,0:T(8,128)(2,1)S(1)}, f32[2,256]{1,0:T(2,128)S(1)}) custom-call(s32[2,256]{1,0:T(2,128)S(1)} %bitcast.4, bf16[2,256]{1,0:T(2,128)(2,1)S(1)} %bitcast.5, bf16[256,3072]{1,0:T(8,128)(2,1)S(1)} %copy-done, bf16[256,3072]{1,0:T(8,128)(2,1)} %dy_ref.1, ...), custom_call_target="tpu_custom_call" | custom-call | flops 5435817984 | bytes 15728640 | tf_op jit(solution)/shard_map/pallas_call | solution.py:340
  179.2 1.1 copy.15
  180.4 1.1 copy.16
  181.5 1.1 copy.17
  182.6 0.6 copy.18
Async XLA Ops:
  0.6 1.4 copy-start
  2.0 0.7 copy-start.1
  2.7 0.7 copy-start.2
